TPU v7x, 512 devices: a whole 4x8x8 slice. The times are simulated.
512 devices in a mesh: dom: 128 (over z, y, core), sub: 4 (over x).
Axes of the slice: x: 4, y: 8, z: 8, core: 2. Of those that a mesh axis runs over, the one named last changes fastest.
Arguments:
- rhs: float32 [64, 8, 65536], P(None, None, ('dom', 'sub')), may hold values from -6 to 6
- guess: float32 [64, 8, 65536], P(None, None, ('dom', 'sub')), may hold values from -4 to 4
- diag_blocks: bfloat16 [2, 64, 64], replicated
- face_blocks: bfloat16 [6, 2, 64, 64], replicated, may hold values from -0.3125 to 0.3125
- smoother: bfloat16 [2, 64, 64], replicated
- coarse_inverse: bfloat16 [64, 64], replicated
- elem_type: int32 [65536], P(('dom', 'sub')), may hold values from 0 to 1
- face_type: int32 [6, 65536], P(None, ('dom', 'sub')), may hold values from 0 to 1
- neighbours: int32 [6, 65536], P(None, ('dom', 'sub')), may hold values from 0 to 239, as said below
- send_near: int32 [2, 16384], P(None, ('dom', 'sub')), may hold values from 0 to 127
- send_far: int32 [2, 4096], P(None, ('dom', 'sub')), may hold values from 0 to 127
- sub_send: int32 [4096], P(('dom', 'sub')), may hold values from 0 to 127
- partner: int32 [65536], P(('dom', 'sub')), may hold values from 0 to 143, as said below
- pair_send: int32 [8192], P(('dom', 'sub')), may hold values from 0 to 127, as said below
Outputs:
- solution: float32 [64, 8, 65536], P(None, None, ('dom', 'sub'))
- residual: float32 [64, 8, 65536], P(None, None, ('dom', 'sub'))
Inputs may be any that keep to these rules, and one draw needn't show every extreme that they name: `neighbours`: values below 128 are the device's own elements; the rest index its 112 received rows in the order of the first step. On each device the partner relation is mutual: local values pair two distinct local elements with each other; each value 128 + q for q below 16 appears exactly once, and the element holding it is entry q of the device's pair_send. `pair_send`: on each device the 16 entries are distinct; slot q pairs with slot q of the device whose sub index differs in the lowest bit.
All inputs are finite; a program needn't handle non-finite values.
Results may differ from a plain program's by a relative error of at most 0.012.
Values may be sent and summed in bfloat16 or wider, within the bound.
No kernel may reach another device: no remote copies, remote signals or barrier semaphores. Data moves between devices by JAX's collectives and lax.ppermute only.
A program may use at most 64 MiB of HBM per device.

v0:
```python
import jax
import jax.numpy as jnp
from jax import lax
from jax.sharding import PartitionSpec as P

SWEEPS = 2


def from_behind(array, axis, by):
    peers = lax.axis_size(axis)
    pairs = [(i, i + by) for i in range(peers) if 0 <= i + by < peers]
    return lax.ppermute(array, axis, pairs)


def partner_2(block, axis, stride):
    count = lax.axis_size(axis)
    route = []
    for low in range(count):
        high = low | 1 << stride
        if high != low and high < count:
            route += [(low, high), (high, low)]
    return lax.ppermute(block, axis, route)


def stack_apply(blocks, field_b, kinds):
    variants = blocks.shape[0]
    node_rows, rhs_width, elements = field_b.shape
    blank = jnp.zeros_like(field_b)
    pieces = [
        jnp.where(kinds[None, None, :] == variant, field_b, blank) for variant in range(variants)
    ]
    operand = jnp.concatenate(pieces, axis=0).reshape(variants * node_rows, rhs_width * elements)
    wide_blocks = jnp.concatenate([blocks[variant] for variant in range(variants)], axis=1)
    product = jnp.dot(wide_blocks, operand, preferred_element_type=jnp.float32)
    return product.reshape(node_rows, rhs_width, elements)


def body(
    rhs,
    guess,
    diag_blocks,
    face_blocks,
    smoother,
    coarse_inverse,
    elem_type,
    face_type,
    neighbours,
    send_near,
    send_far,
    sub_send,
    partner,
    pair_send,
):

    def apply_local(field_b):
        up_near = jnp.take(field_b, send_near[1], axis=2)
        down_near = jnp.take(field_b, send_near[0], axis=2)
        up_far = jnp.take(field_b, send_far[1], axis=2)
        down_far = jnp.take(field_b, send_far[0], axis=2)
        from_below = from_behind(up_near, "dom", 1)
        from_above = from_behind(down_near, "dom", -1)
        far_below = from_behind(up_far, "dom", 2)
        far_above = from_behind(down_far, "dom", -2)
        side_rows = lax.all_gather(jnp.take(field_b, sub_send, axis=2), "sub", axis=2, tiled=True)
        extended = jnp.concatenate(
            [field_b, from_below, from_above, far_below, far_above, side_rows], axis=2
        )
        total = stack_apply(diag_blocks, field_b, elem_type)
        for face_index in range(6):
            beside = jnp.take(extended, neighbours[face_index], axis=2)
            total = total + stack_apply(face_blocks[face_index], beside, face_type[face_index])
        return total

    iterate = guess
    for rounds in range(SWEEPS):
        sweep_res = rhs - apply_local(iterate.astype(jnp.bfloat16))
        iterate = iterate + stack_apply(smoother, sweep_res.astype(jnp.bfloat16), elem_type)
    residual = rhs - apply_local(iterate.astype(jnp.bfloat16))
    outgoing = jnp.take(residual, pair_send, axis=2)
    incoming = partner_2(outgoing.astype(jnp.bfloat16), "sub", 0).astype(outgoing.dtype)
    joined = jnp.concatenate([residual, incoming], axis=2)
    coarse = residual + jnp.take(joined, partner, axis=2)
    node_rows, rhs_width, elements = coarse.shape
    coarse_b = coarse.astype(jnp.bfloat16).reshape(node_rows, rhs_width * elements)
    update = jnp.dot(coarse_inverse, coarse_b, preferred_element_type=jnp.float32)
    solution = iterate + update.reshape(node_rows, rhs_width, elements)
    return (solution, residual)


def solution(mesh):
    in_specs = (
        P(None, None, ("dom", "sub")),
        P(None, None, ("dom", "sub")),
        P(),
        P(),
        P(),
        P(),
        P(("dom", "sub")),
        P(None, ("dom", "sub")),
        P(None, ("dom", "sub")),
        P(None, ("dom", "sub")),
        P(None, ("dom", "sub")),
        P(("dom", "sub")),
        P(("dom", "sub")),
        P(("dom", "sub")),
    )
    out_specs = (P(None, None, ("dom", "sub")), P(None, None, ("dom", "sub")))
    return jax.shard_map(body, mesh=mesh, in_specs=in_specs, out_specs=out_specs, check_vma=False)
```

profile of v0, /device:TPU:256, one launch (start us, length us, event | category | flops | bytes accessed | tf_op | source)
XLA Modules:
  0.0 147.1 jit_solution(16618105193743809623)
XLA Ops:
  1.3 1.0 broadcast_select_fusion.27
  3.3 1.9 %collective-permute-start = (bf16[64,8,32]{2,0,1:T(8,128)(2,1)S(1)}, bf16[64,8,32]{2,0,1:T(8,128)(2,1)S(1)}, u32[]{:S(2)}, u32[]{:S(2)}) collective-permute-start(bf16[64,8,32]{2,0,1:T(8,128)(2,1)S(1)} %select_bitcast_fusion.5), channel_id=1, source_target_pairs={{0,4},{4,8},{8,12},{12,16},{16,20},{20,24},{24,28},{28,32},{32,36}... | collective-permute-start | bytes 98312 | tf_op jit(solution)/shard_map/ppermute | solution.py:12
  6.1 7.0 %collective-permute-start.1 = (bf16[64,8,32]{2,0,1:T(8,128)(2,1)S(1)}, bf16[64,8,32]{2,0,1:T(8,128)(2,1)S(1)}, u32[]{:S(2)}, u32[]{:S(2)}) collective-permute-start(bf16[64,8,32]{2,0,1:T(8,128)(2,1)S(1)} %select_bitcast_fusion.4), channel_id=1, source_target_pairs={{4,0},{8,4},{12,8},{16,12},{20,16},{24,20},{28,24},{32,28},{36,32}... | collective-permute-start | bytes 98312 | tf_op jit(solution)/shard_map/ppermute | solution.py:12
  13.7 1.9 %collective-permute-start.2 = (bf16[64,8,8]{0,1,2:T(8,128)(2,1)S(1)}, bf16[64,8,8]{0,1,2:T(8,128)(2,1)S(1)}, u32[]{:S(2)}, u32[]{:S(2)}) collective-permute-start(bf16[64,8,8]{0,1,2:T(8,128)(2,1)S(1)} %select_bitcast_fusion.14), channel_id=1, source_target_pairs={{0,8},{4,12},{8,16},{12,20},{16,24},{20,28},{24,32},{28,36},{32,40... | collective-permute-start | bytes 24584 | tf_op jit(solution)/shard_map/ppermute | solution.py:12
  16.3 7.2 %collective-permute-start.3 = (bf16[64,8,8]{0,1,2:T(8,128)(2,1)S(1)}, bf16[64,8,8]{0,1,2:T(8,128)(2,1)S(1)}, u32[]{:S(2)}, u32[]{:S(2)}) collective-permute-start(bf16[64,8,8]{0,1,2:T(8,128)(2,1)S(1)} %select_bitcast_fusion.13), channel_id=1, source_target_pairs={{8,0},{12,4},{16,8},{20,12},{24,16},{28,20},{32,24},{36,28},{40,32... | collective-permute-start | bytes 24584 | tf_op jit(solution)/shard_map/ppermute | solution.py:12
  25.6 12.2 %all_gather.9 = bf16[64,8,32]{0,1,2:T(8,128)(2,1)S(1)} all-gather(bf16[64,8,8]{0,1,2:T(8,128)(2,1)S(1)} %select_bitcast_fusion.12), channel_id=1, replica_groups=mesh['dom'=128,'sub'=4] {'sub'}, dimensions={2}, use_global_device_ids=true | all-gather | bytes 40960 | tf_op jit(solution)/shard_map/all_gather | solution.py:64
  38.8 0.7 gather_fusion.7
  40.0 0.7 gather_fusion.8
  41.1 0.7 gather_fusion.9
  42.2 0.7 gather_fusion.10
  43.4 0.7 gather_fusion.11
  44.5 0.7 gather_fusion.12
  48.2 0.7 copy-done.2
  52.9 1.9 %collective-permute-start.4 = (bf16[64,8,32]{2,0,1:T(8,128)(2,1)S(1)}, bf16[64,8,32]{2,0,1:T(8,128)(2,1)S(1)}, u32[]{:S(2)}, u32[]{:S(2)}) collective-permute-start(bf16[64,8,32]{2,0,1:T(8,128)(2,1)S(1)} %select_bitcast_fusion.3), channel_id=1, source_target_pairs={{0,4},{4,8},{8,12},{12,16},{16,20},{20,24},{24,28},{28,32},{32,36}... | collective-permute-start | bytes 98312 | tf_op jit(solution)/shard_map/ppermute | solution.py:12
  55.0 7.0 %collective-permute-start.5 = (bf16[64,8,32]{2,0,1:T(8,128)(2,1)S(1)}, bf16[64,8,32]{2,0,1:T(8,128)(2,1)S(1)}, u32[]{:S(2)}, u32[]{:S(2)}) collective-permute-start(bf16[64,8,32]{2,0,1:T(8,128)(2,1)S(1)} %select_bitcast_fusion.2), channel_id=1, source_target_pairs={{4,0},{8,4},{12,8},{16,12},{20,16},{24,20},{28,24},{32,28},{36,32}... | collective-permute-start | bytes 98312 | tf_op jit(solution)/shard_map/ppermute | solution.py:12
  62.1 1.9 %collective-permute-start.6 = (bf16[64,8,8]{0,1,2:T(8,128)(2,1)S(1)}, bf16[64,8,8]{0,1,2:T(8,128)(2,1)S(1)}, u32[]{:S(2)}, u32[]{:S(2)}) collective-permute-start(bf16[64,8,8]{0,1,2:T(8,128)(2,1)S(1)} %select_bitcast_fusion.11), channel_id=1, source_target_pairs={{0,8},{4,12},{8,16},{12,20},{16,24},{20,28},{24,32},{28,36},{32,40... | collective-permute-start | bytes 24584 | tf_op jit(solution)/shard_map/ppermute | solution.py:12
  64.1 7.2 %collective-permute-start.7 = (bf16[64,8,8]{0,1,2:T(8,128)(2,1)S(1)}, bf16[64,8,8]{0,1,2:T(8,128)(2,1)S(1)}, u32[]{:S(2)}, u32[]{:S(2)}) collective-permute-start(bf16[64,8,8]{0,1,2:T(8,128)(2,1)S(1)} %select_bitcast_fusion.10), channel_id=1, source_target_pairs={{8,0},{12,4},{16,8},{20,12},{24,16},{28,20},{32,24},{36,28},{40,32... | collective-permute-start | bytes 24584 | tf_op jit(solution)/shard_map/ppermute | solution.py:12
  71.4 12.0 %all_gather.10 = bf16[64,8,32]{0,1,2:T(8,128)(2,1)S(1)} all-gather(bf16[64,8,8]{0,1,2:T(8,128)(2,1)S(1)} %select_bitcast_fusion.9), channel_id=1, replica_groups=mesh['dom'=128,'sub'=4] {'sub'}, dimensions={2}, use_global_device_ids=true | all-gather | bytes 40960 | tf_op jit(solution)/shard_map/all_gather | solution.py:64
  84.5 0.7 gather_fusion.18
  87.2 0.7 gather_fusion.22
  97.1 1.9 %collective-permute-start.8 = (bf16[64,8,32]{2,0,1:T(8,128)(2,1)S(1)}, bf16[64,8,32]{2,0,1:T(8,128)(2,1)S(1)}, u32[]{:S(2)}, u32[]{:S(2)}) collective-permute-start(bf16[64,8,32]{2,0,1:T(8,128)(2,1)S(1)} %select_bitcast_fusion.1), channel_id=1, source_target_pairs={{0,4},{4,8},{8,12},{12,16},{16,20},{20,24},{24,28},{28,32},{32,36}... | collective-permute-start | bytes 98312 | tf_op jit(solution)/shard_map/ppermute | solution.py:12
  99.2 7.0 %collective-permute-start.9 = (bf16[64,8,32]{2,0,1:T(8,128)(2,1)S(1)}, bf16[64,8,32]{2,0,1:T(8,128)(2,1)S(1)}, u32[]{:S(2)}, u32[]{:S(2)}) collective-permute-start(bf16[64,8,32]{2,0,1:T(8,128)(2,1)S(1)} %select_bitcast_fusion), channel_id=1, source_target_pairs={{4,0},{8,4},{12,8},{16,12},{20,16},{24,20},{28,24},{32,28},{36,32}... | collective-permute-start | bytes 98312 | tf_op jit(solution)/shard_map/ppermute | solution.py:12
  106.3 1.9 %collective-permute-start.10 = (bf16[64,8,8]{0,1,2:T(8,128)(2,1)S(1)}, bf16[64,8,8]{0,1,2:T(8,128)(2,1)S(1)}, u32[]{:S(2)}, u32[]{:S(2)}) collective-permute-start(bf16[64,8,8]{0,1,2:T(8,128)(2,1)S(1)} %select_bitcast_fusion.8), channel_id=1, source_target_pairs={{0,8},{4,12},{8,16},{12,20},{16,24},{20,28},{24,32},{28,36},{32,40... | collective-permute-start | bytes 24584 | tf_op jit(solution)/shard_map/ppermute | solution.py:12
  108.3 7.2 %collective-permute-start.11 = (bf16[64,8,8]{0,1,2:T(8,128)(2,1)S(1)}, bf16[64,8,8]{0,1,2:T(8,128)(2,1)S(1)}, u32[]{:S(2)}, u32[]{:S(2)}) collective-permute-start(bf16[64,8,8]{0,1,2:T(8,128)(2,1)S(1)} %select_bitcast_fusion.7), channel_id=1, source_target_pairs={{8,0},{12,4},{16,8},{20,12},{24,16},{28,20},{32,24},{36,28},{40,32... | collective-permute-start | bytes 24584 | tf_op jit(solution)/shard_map/ppermute | solution.py:12
  115.6 11.9 %all_gather.11 = bf16[64,8,32]{0,1,2:T(8,128)(2,1)S(1)} all-gather(bf16[64,8,8]{0,1,2:T(8,128)(2,1)S(1)} %select_bitcast_fusion.6), channel_id=1, replica_groups=mesh['dom'=128,'sub'=4] {'sub'}, dimensions={2}, use_global_device_ids=true | all-gather | bytes 40960 | tf_op jit(solution)/shard_map/all_gather | solution.py:64
  129.2 0.7 gather_fusion.29
  132.0 0.7 gather_fusion.33
  137.9 3.1 %collective-permute-start.12 = (bf16[64,8,16]{2,0,1:T(8,128)(2,1)S(1)}, bf16[64,8,16]{2,0,1:T(8,128)(2,1)S(1)}, u32[]{:S(2)}, u32[]{:S(2)}) collective-permute-start(bf16[64,8,16]{2,0,1:T(8,128)(2,1)S(1)} %fusion.32), channel_id=1, source_target_pairs={{0,1},{1,0},{2,3},{3,2},{4,5},{5,4},{6,7},{7,6},{8,9},{9,8},{10,11... | collective-permute-start | bytes 49160 | tf_op jit(solution)/shard_map/ppermute | solution.py:22
  140.9 0.9 copy.358
  141.8 2.9 %collective-permute-done.12 = bf16[64,8,16]{2,0,1:T(8,128)(2,1)S(1)} collective-permute-done((bf16[64,8,16]{2,0,1:T(8,128)(2,1)S(1)}, bf16[64,8,16]{2,0,1:T(8,128)(2,1)S(1)}, u32[]{:S(2)}, u32[]{:S(2)}) %collective-permute-start.12) | collective-permute-done | bytes 16416 | tf_op jit(solution)/shard_map/ppermute | solution.py:22
  145.1 0.8 gather_fusion.1
  146.3 0.9 copy.357
  (241 shorter events, 37.7 us)
Async XLA Ops:
  0.6 145.4 %copy-start = (bf16[64,64]{1,0:T(8,128)(2,1)S(1)}, bf16[64,64]{1,0:T(8,128)(2,1)}, u32[]{:S(2)}) copy-start(bf16[64,64]{1,0:T(8,128)(2,1)} %param.25) | copy-start | bytes 24580
  0.6 1.9 %copy-start.8 = (s32[2,32]{1,0:T(2,128)S(1)}, s32[2,32]{1,0:T(2,128)}, u32[]{:S(2)}) copy-start(s32[2,32]{1,0:T(2,128)} %param.29) | copy-start | bytes 772
  3.2 9.9 %copy-start.9 = (s32[2,8]{1,0:T(2,128)S(1)}, s32[2,8]{1,0:T(2,128)}, u32[]{:S(2)}) copy-start(s32[2,8]{1,0:T(2,128)} %param.30) | copy-start | bytes 196
  3.3 34.9 %collective-permute-start = (bf16[64,8,32]{2,0,1:T(8,128)(2,1)S(1)}, bf16[64,8,32]{2,0,1:T(8,128)(2,1)S(1)}, u32[]{:S(2)}, u32[]{:S(2)}) collective-permute-start(bf16[64,8,32]{2,0,1:T(8,128)(2,1)S(1)} %select_bitcast_fusion.5), channel_id=1, source_target_pairs={{0,4},{4,8},{8,12},{12,16},{16,20},{20,24},{24,28},{28,32},{32,36}... | collective-permute-start | bytes 98312 | tf_op jit(solution)/shard_map/ppermute | solution.py:12
  5.9 17.7 %copy-start.10 = (s32[8]{0:T(128)S(1)}, s32[8]{0:T(128)}, u32[]{:S(2)}) copy-start(s32[8]{0:T(128)} %param.31) | copy-start | bytes 100
  5.9 17.7 %copy-start.11 = (s32[16]{0:T(128)S(1)}, s32[16]{0:T(128)}, u32[]{:S(2)}) copy-start(s32[16]{0:T(128)} %param.33) | copy-start | bytes 196
  5.9 17.7 %copy-start.12 = (s32[128]{0:T(128)S(1)}, s32[128]{0:T(128)}, u32[]{:S(2)}) copy-start(s32[128]{0:T(128)} %param.32) | copy-start | bytes 1540
  6.1 32.2 %collective-permute-start.1 = (bf16[64,8,32]{2,0,1:T(8,128)(2,1)S(1)}, bf16[64,8,32]{2,0,1:T(8,128)(2,1)S(1)}, u32[]{:S(2)}, u32[]{:S(2)}) collective-permute-start(bf16[64,8,32]{2,0,1:T(8,128)(2,1)S(1)} %select_bitcast_fusion.4), channel_id=1, source_target_pairs={{4,0},{8,4},{12,8},{16,12},{20,16},{24,20},{28,24},{32,28},{36,32}... | collective-permute-start | bytes 98312 | tf_op jit(solution)/shard_map/ppermute | solution.py:12
  13.7 24.2 %collective-permute-start.2 = (bf16[64,8,8]{0,1,2:T(8,128)(2,1)S(1)}, bf16[64,8,8]{0,1,2:T(8,128)(2,1)S(1)}, u32[]{:S(2)}, u32[]{:S(2)}) collective-permute-start(bf16[64,8,8]{0,1,2:T(8,128)(2,1)S(1)} %select_bitcast_fusion.14), channel_id=1, source_target_pairs={{0,8},{4,12},{8,16},{12,20},{16,24},{20,28},{24,32},{28,36},{32,40... | collective-permute-start | bytes 24584 | tf_op jit(solution)/shard_map/ppermute | solution.py:12
  16.3 21.8 %collective-permute-start.3 = (bf16[64,8,8]{0,1,2:T(8,128)(2,1)S(1)}, bf16[64,8,8]{0,1,2:T(8,128)(2,1)S(1)}, u32[]{:S(2)}, u32[]{:S(2)}) collective-permute-start(bf16[64,8,8]{0,1,2:T(8,128)(2,1)S(1)} %select_bitcast_fusion.13), channel_id=1, source_target_pairs={{8,0},{12,4},{16,8},{20,12},{24,16},{28,20},{32,24},{36,28},{40,32... | collective-permute-start | bytes 24584 | tf_op jit(solution)/shard_map/ppermute | solution.py:12
  23.7 0.8 copy-start.4
  23.7 0.8 copy-start.6
  23.7 1.3 copy-start.7
  23.7 1.4 copy-start.3
  23.8 1.4 copy-start.5
  46.7 1.0 copy-start.1
  48.0 1.0 copy-start.2
  52.9 30.9 %collective-permute-start.4 = (bf16[64,8,32]{2,0,1:T(8,128)(2,1)S(1)}, bf16[64,8,32]{2,0,1:T(8,128)(2,1)S(1)}, u32[]{:S(2)}, u32[]{:S(2)}) collective-permute-start(bf16[64,8,32]{2,0,1:T(8,128)(2,1)S(1)} %select_bitcast_fusion.3), channel_id=1, source_target_pairs={{0,4},{4,8},{8,12},{12,16},{16,20},{20,24},{24,28},{28,32},{32,36}... | collective-permute-start | bytes 98312 | tf_op jit(solution)/shard_map/ppermute | solution.py:12
  55.0 28.9 %collective-permute-start.5 = (bf16[64,8,32]{2,0,1:T(8,128)(2,1)S(1)}, bf16[64,8,32]{2,0,1:T(8,128)(2,1)S(1)}, u32[]{:S(2)}, u32[]{:S(2)}) collective-permute-start(bf16[64,8,32]{2,0,1:T(8,128)(2,1)S(1)} %select_bitcast_fusion.2), channel_id=1, source_target_pairs={{4,0},{8,4},{12,8},{16,12},{20,16},{24,20},{28,24},{32,28},{36,32}... | collective-permute-start | bytes 98312 | tf_op jit(solution)/shard_map/ppermute | solution.py:12
  62.1 21.5 %collective-permute-start.6 = (bf16[64,8,8]{0,1,2:T(8,128)(2,1)S(1)}, bf16[64,8,8]{0,1,2:T(8,128)(2,1)S(1)}, u32[]{:S(2)}, u32[]{:S(2)}) collective-permute-start(bf16[64,8,8]{0,1,2:T(8,128)(2,1)S(1)} %select_bitcast_fusion.11), channel_id=1, source_target_pairs={{0,8},{4,12},{8,16},{12,20},{16,24},{20,28},{24,32},{28,36},{32,40... | collective-permute-start | bytes 24584 | tf_op jit(solution)/shard_map/ppermute | solution.py:12
  64.1 19.6 %collective-permute-start.7 = (bf16[64,8,8]{0,1,2:T(8,128)(2,1)S(1)}, bf16[64,8,8]{0,1,2:T(8,128)(2,1)S(1)}, u32[]{:S(2)}, u32[]{:S(2)}) collective-permute-start(bf16[64,8,8]{0,1,2:T(8,128)(2,1)S(1)} %select_bitcast_fusion.10), channel_id=1, source_target_pairs={{8,0},{12,4},{16,8},{20,12},{24,16},{28,20},{32,24},{36,28},{40,32... | collective-permute-start | bytes 24584 | tf_op jit(solution)/shard_map/ppermute | solution.py:12
  97.1 30.8 %collective-permute-start.8 = (bf16[64,8,32]{2,0,1:T(8,128)(2,1)S(1)}, bf16[64,8,32]{2,0,1:T(8,128)(2,1)S(1)}, u32[]{:S(2)}, u32[]{:S(2)}) collective-permute-start(bf16[64,8,32]{2,0,1:T(8,128)(2,1)S(1)} %select_bitcast_fusion.1), channel_id=1, source_target_pairs={{0,4},{4,8},{8,12},{12,16},{16,20},{20,24},{24,28},{28,32},{32,36}... | collective-permute-start | bytes 98312 | tf_op jit(solution)/shard_map/ppermute | solution.py:12
  99.2 28.7 %collective-permute-start.9 = (bf16[64,8,32]{2,0,1:T(8,128)(2,1)S(1)}, bf16[64,8,32]{2,0,1:T(8,128)(2,1)S(1)}, u32[]{:S(2)}, u32[]{:S(2)}) collective-permute-start(bf16[64,8,32]{2,0,1:T(8,128)(2,1)S(1)} %select_bitcast_fusion), channel_id=1, source_target_pairs={{4,0},{8,4},{12,8},{16,12},{20,16},{24,20},{28,24},{32,28},{36,32}... | collective-permute-start | bytes 98312 | tf_op jit(solution)/shard_map/ppermute | solution.py:12
  106.3 21.3 %collective-permute-start.10 = (bf16[64,8,8]{0,1,2:T(8,128)(2,1)S(1)}, bf16[64,8,8]{0,1,2:T(8,128)(2,1)S(1)}, u32[]{:S(2)}, u32[]{:S(2)}) collective-permute-start(bf16[64,8,8]{0,1,2:T(8,128)(2,1)S(1)} %select_bitcast_fusion.8), channel_id=1, source_target_pairs={{0,8},{4,12},{8,16},{12,20},{16,24},{20,28},{24,32},{28,36},{32,40... | collective-permute-start | bytes 24584 | tf_op jit(solution)/shard_map/ppermute | solution.py:12
  108.3 19.5 %collective-permute-start.11 = (bf16[64,8,8]{0,1,2:T(8,128)(2,1)S(1)}, bf16[64,8,8]{0,1,2:T(8,128)(2,1)S(1)}, u32[]{:S(2)}, u32[]{:S(2)}) collective-permute-start(bf16[64,8,8]{0,1,2:T(8,128)(2,1)S(1)} %select_bitcast_fusion.7), channel_id=1, source_target_pairs={{8,0},{12,4},{16,8},{20,12},{24,16},{28,20},{32,24},{36,28},{40,32... | collective-permute-start | bytes 24584 | tf_op jit(solution)/shard_map/ppermute | solution.py:12
  137.9 6.9 %collective-permute-start.12 = (bf16[64,8,16]{2,0,1:T(8,128)(2,1)S(1)}, bf16[64,8,16]{2,0,1:T(8,128)(2,1)S(1)}, u32[]{:S(2)}, u32[]{:S(2)}) collective-permute-start(bf16[64,8,16]{2,0,1:T(8,128)(2,1)S(1)} %fusion.32), channel_id=1, source_target_pairs={{0,1},{1,0},{2,3},{3,2},{4,5},{5,4},{6,7},{7,6},{8,9},{9,8},{10,11... | collective-permute-start | bytes 49160 | tf_op jit(solution)/shard_map/ppermute | solution.py:22
where the time goes:
time: 148 us; the launch traced here: 147 us
  starting transfers between devices  57.2 us (39%)
  local copies, waits for them, and re-layouts  39 us (26%)
  blocking collectives  36.1 us (24%)
  matrix products  6.08 us (4%)
  other arithmetic  3.72 us (3%)
  waiting for transfers between devices  2.94 us (2%)
  between operations  2.13 us (1%)
    ppermute x12, starting transfers between devices, from_behind(): return lax.ppermute(array, axis, pairs)  54.1 us
    all_gather x3, blocking collectives, apply_local(): lax.all_gather(jnp.take(field_b, sub_send, axis=2), 'sub', axis=2, tiled=...  36.1 us
    gather x36, local copies, waits for them, and re-layouts, apply_local(): beside = jnp.take(extended, neighbours[face_index], axis=2)  16.1 us
    dot_general x23, matrix products, stack_apply(): product = jnp.dot(wide_blocks, operand, preferred_element_type=jnp.float32)  5.91 us
    concatenate x23, local copies, waits for them, and re-layouts, stack_apply(): jnp.concatenate(pieces, axis=0)  4.08 us
    unnamed x28, local copies, waits for them, and re-layouts  3.7 us
    ppermute x1, starting transfers between devices, partner_2(): return lax.ppermute(block, axis, route)  3.07 us
  transfers between devices with their start and end apart: 13, of which 1 were waited for; matrix products, arithmetic and copies ran while one was open for 4% of the time, Pallas kernels for 0%

commit v1 on v0

--- a/solution.py
+++ b/solution.py
@@ -61,7 +61,25 @@
         from_above = from_behind(down_near, "dom", -1)
         far_below = from_behind(up_far, "dom", 2)
         far_above = from_behind(down_far, "dom", -2)
-        side_rows = lax.all_gather(jnp.take(field_b, sub_send, axis=2), "sub", axis=2, tiled=True)
+        x = jnp.take(field_b, sub_send, axis=2)
+        size, here, extent = (lax.axis_size("sub"), lax.axis_index("sub"), x.shape[2])
+        forward = [(i_2, (i_2 + 1) % size) for i_2 in range(size)]
+        downward = [(i_2, (i_2 - 1) % size) for i_2 in range(size)]
+        filled = jnp.zeros((*x.shape[:2], size * extent, *x.shape[2 + 1 :]), x.dtype)
+        filled = lax.dynamic_update_slice_in_dim(filled, x, here * extent, axis=2)
+        from_left = from_right = x
+        halfway = size // 2
+        for step in range(1, halfway + 1):
+            from_left = lax.ppermute(from_left, "sub", forward)
+            filled = lax.dynamic_update_slice_in_dim(
+                filled, from_left, (here - step) % size * extent, axis=2
+            )
+            if step < size - halfway:
+                from_right = lax.ppermute(from_right, "sub", downward)
+                filled = lax.dynamic_update_slice_in_dim(
+                    filled, from_right, (here + step) % size * extent, axis=2
+                )
+        side_rows = filled
         extended = jnp.concatenate(
             [field_b, from_below, from_above, far_below, far_above, side_rows], axis=2
         )

time: 148 us -> 160 us (1.081)
  the two profiles are of different devices: /device:TPU:256 before, /device:TPU:262 now
where the time goes in v1:
time: 160 us; the launch traced here: 159 us
  starting transfers between devices  84.9 us (53%)
  local copies, waits for them, and re-layouts  57.3 us (36%)
  matrix products  6.08 us (4%)
  other arithmetic  5.04 us (3%)
  waiting for transfers between devices  3.56 us (2%)
  between operations  2.45 us (2%)
    ppermute x12, starting transfers between devices, from_behind(): return lax.ppermute(array, axis, pairs)  54.1 us
    ppermute x6, starting transfers between devices, apply_local(): from_left = lax.ppermute(from_left, 'sub', forward)  17.5 us
    gather x36, local copies, waits for them, and re-layouts, apply_local(): beside = jnp.take(extended, neighbours[face_index], axis=2)  16 us
    ppermute x3, starting transfers between devices, apply_local(): from_right = lax.ppermute(from_right, 'sub', downward)  10.8 us
    dynamic_update_slice x6, local copies, waits for them, and re-layouts, apply_local(): lax.dynamic_update_slice_in_dim(filled, from_left, (here - step) % size *...  10.5 us
    dot_general x23, matrix products, stack_apply(): product = jnp.dot(wide_blocks, operand, preferred_element_type=jnp.float32)  5.91 us
    dynamic_update_slice x3, local copies, waits for them, and re-layouts, apply_local(): filled = lax.dynamic_update_slice_in_dim(filled, x, here * extent, axis=2)  5.25 us
    concatenate x23, local copies, waits for them, and re-layouts, stack_apply(): jnp.concatenate(pieces, axis=0)  4.08 us
  transfers between devices with their start and end apart: 22, of which 1 were waited for; matrix products, arithmetic and copies ran while one was open for 16% of the time, Pallas kernels for 0%

profile of v1, /device:TPU:262, one launch (start us, length us, event | category | flops | bytes accessed | tf_op | source)
XLA Modules:
  0.0 159.4 jit_solution(13728540013435692968)
XLA Ops:
  4.5 2.4 %collective-permute-start.4 = (bf16[64,8,8]{0,1,2:T(8,128)(2,1)S(1)}, bf16[64,8,8]{0,1,2:T(8,128)(2,1)S(1)}, u32[]{:S(2)}, u32[]{:S(2)}) collective-permute-start(bf16[64,8,8]{0,1,2:T(8,128)(2,1)S(1)} %select_bitcast_fusion.12), channel_id=1, source_target_pairs={{0,1},{1,2},{2,3},{3,0},{4,5},{5,6},{6,7},{7,4},{8,9},{9,10},{10,1... | collective-permute-start | bytes 24584 | tf_op jit(solution)/shard_map/ppermute | solution.py:73
  6.9 3.5 %collective-permute-start.5 = (bf16[64,8,8]{0,1,2:T(8,128)(2,1)S(1)}, bf16[64,8,8]{0,1,2:T(8,128)(2,1)S(1)}, u32[]{:S(2)}, u32[]{:S(2)}) collective-permute-start(bf16[64,8,8]{0,1,2:T(8,128)(2,1)S(1)} %select_bitcast_fusion.12), channel_id=1, source_target_pairs={{0,3},{1,0},{2,1},{3,2},{4,7},{5,4},{6,5},{7,6},{8,11},{9,8},{10,9... | collective-permute-start | bytes 24584 | tf_op jit(solution)/shard_map/ppermute | solution.py:78
  11.2 1.9 %collective-permute-start = (bf16[64,8,32]{2,0,1:T(8,128)(2,1)S(1)}, bf16[64,8,32]{2,0,1:T(8,128)(2,1)S(1)}, u32[]{:S(2)}, u32[]{:S(2)}) collective-permute-start(bf16[64,8,32]{2,0,1:T(8,128)(2,1)S(1)} %select_bitcast_fusion.5), channel_id=1, source_target_pairs={{0,4},{4,8},{8,12},{12,16},{16,20},{20,24},{24,28},{28,32},{32,36}... | collective-permute-start | bytes 98312 | tf_op jit(solution)/shard_map/ppermute | solution.py:12
  13.9 7.0 %collective-permute-start.1 = (bf16[64,8,32]{2,0,1:T(8,128)(2,1)S(1)}, bf16[64,8,32]{2,0,1:T(8,128)(2,1)S(1)}, u32[]{:S(2)}, u32[]{:S(2)}) collective-permute-start(bf16[64,8,32]{2,0,1:T(8,128)(2,1)S(1)} %select_bitcast_fusion.4), channel_id=1, source_target_pairs={{4,0},{8,4},{12,8},{16,12},{20,16},{24,20},{28,24},{32,28},{36,32}... | collective-permute-start | bytes 98312 | tf_op jit(solution)/shard_map/ppermute | solution.py:12
  21.5 1.9 %collective-permute-start.2 = (bf16[64,8,8]{0,1,2:T(8,128)(2,1)S(1)}, bf16[64,8,8]{0,1,2:T(8,128)(2,1)S(1)}, u32[]{:S(2)}, u32[]{:S(2)}) collective-permute-start(bf16[64,8,8]{0,1,2:T(8,128)(2,1)S(1)} %select_bitcast_fusion.14), channel_id=1, source_target_pairs={{0,8},{4,12},{8,16},{12,20},{16,24},{20,28},{24,32},{28,36},{32,40... | collective-permute-start | bytes 24584 | tf_op jit(solution)/shard_map/ppermute | solution.py:12
  25.4 7.2 %collective-permute-start.3 = (bf16[64,8,8]{0,1,2:T(8,128)(2,1)S(1)}, bf16[64,8,8]{0,1,2:T(8,128)(2,1)S(1)}, u32[]{:S(2)}, u32[]{:S(2)}) collective-permute-start(bf16[64,8,8]{0,1,2:T(8,128)(2,1)S(1)} %select_bitcast_fusion.13), channel_id=1, source_target_pairs={{8,0},{12,4},{16,8},{20,12},{24,16},{28,20},{32,24},{36,28},{40,32... | collective-permute-start | bytes 24584 | tf_op jit(solution)/shard_map/ppermute | solution.py:12
  32.7 3.6 %collective-permute-start.6 = (bf16[64,8,8]{0,1,2:T(8,128)(2,1)S(1)}, bf16[64,8,8]{0,1,2:T(8,128)(2,1)S(1)}, u32[]{:S(2)}, u32[]{:S(2)}) collective-permute-start(bf16[64,8,8]{0,1,2:T(8,128)(2,1)S(1)} %collective-permute-done.4), channel_id=1, source_target_pairs={{0,1},{1,2},{2,3},{3,0},{4,5},{5,6},{6,7},{7,4},{8,9},{9,10},{10,1... | collective-permute-start | bytes 24584 | tf_op jit(solution)/shard_map/ppermute | solution.py:73
  36.5 1.8 %dynamic_update_slice.36 = bf16[64,8,32]{2,0,1:T(8,128)(2,1)S(1)} dynamic-update-slice(bf16[64,8,32]{2,0,1:T(8,128)(2,1)S(1)} %broadcast.134.clone, bf16[64,8,8]{2,0,1:T(8,128)(2,1)S(1)} %copy.152, s32[]{:T(128)} %constant.98.clone.1, s32[]{:T(128)} %constant.98.clone.1, s32[]{:T(128)S(6)} %select_n.226) | dynamic-update-slice | bytes 16388 | tf_op jit(solution)/shard_map/dynamic_update_slice | solution.py:69
  38.4 1.8 %dynamic_update_slice.37 = bf16[64,8,32]{2,0,1:T(8,128)(2,1)S(1)} dynamic-update-slice(bf16[64,8,32]{2,0,1:T(8,128)(2,1)S(1)} %dynamic_update_slice.36, bf16[64,8,8]{2,0,1:T(8,128)(2,1)S(1)} %copy.153, s32[]{:T(128)} %constant.98.clone.1, s32[]{:T(128)} %constant.98.clone.1, s32[]{:T(128)S(6)} %select_n.228) | dynamic-update-slice | bytes 16388 | tf_op jit(solution)/shard_map/dynamic_update_slice | solution.py:74
  41.2 1.8 %dynamic_update_slice.39 = bf16[64,8,32]{2,0,1:T(8,128)(2,1)S(1)} dynamic-update-slice(bf16[64,8,32]{2,0,1:T(8,128)(2,1)S(1)} %dynamic_update_slice.38, bf16[64,8,8]{2,0,1:T(8,128)(2,1)S(1)} %copy.155, s32[]{:T(128)} %constant.98.clone.1, s32[]{:T(128)} %constant.98.clone.1, s32[]{:T(128)S(6)} %select_n.232) | dynamic-update-slice | bytes 16388 | tf_op jit(solution)/shard_map/dynamic_update_slice | solution.py:74
  57.2 2.2 %collective-permute-start.11 = (bf16[64,8,8]{0,1,2:T(8,128)(2,1)S(1)}, bf16[64,8,8]{0,1,2:T(8,128)(2,1)S(1)}, u32[]{:S(2)}, u32[]{:S(2)}) collective-permute-start(bf16[64,8,8]{0,1,2:T(8,128)(2,1)S(1)} %select_bitcast_fusion.9), channel_id=1, source_target_pairs={{0,1},{1,2},{2,3},{3,0},{4,5},{5,6},{6,7},{7,4},{8,9},{9,10},{10,1... | collective-permute-start | bytes 24584 | tf_op jit(solution)/shard_map/ppermute | solution.py:73
  59.4 3.6 %collective-permute-start.12 = (bf16[64,8,8]{0,1,2:T(8,128)(2,1)S(1)}, bf16[64,8,8]{0,1,2:T(8,128)(2,1)S(1)}, u32[]{:S(2)}, u32[]{:S(2)}) collective-permute-start(bf16[64,8,8]{0,1,2:T(8,128)(2,1)S(1)} %select_bitcast_fusion.9), channel_id=1, source_target_pairs={{0,3},{1,0},{2,1},{3,2},{4,7},{5,4},{6,5},{7,6},{8,11},{9,8},{10,9... | collective-permute-start | bytes 24584 | tf_op jit(solution)/shard_map/ppermute | solution.py:78
  63.2 1.9 %collective-permute-start.7 = (bf16[64,8,32]{2,0,1:T(8,128)(2,1)S(1)}, bf16[64,8,32]{2,0,1:T(8,128)(2,1)S(1)}, u32[]{:S(2)}, u32[]{:S(2)}) collective-permute-start(bf16[64,8,32]{2,0,1:T(8,128)(2,1)S(1)} %select_bitcast_fusion.3), channel_id=1, source_target_pairs={{0,4},{4,8},{8,12},{12,16},{16,20},{20,24},{24,28},{28,32},{32,36}... | collective-permute-start | bytes 98312 | tf_op jit(solution)/shard_map/ppermute | solution.py:12
  65.3 7.0 %collective-permute-start.8 = (bf16[64,8,32]{2,0,1:T(8,128)(2,1)S(1)}, bf16[64,8,32]{2,0,1:T(8,128)(2,1)S(1)}, u32[]{:S(2)}, u32[]{:S(2)}) collective-permute-start(bf16[64,8,32]{2,0,1:T(8,128)(2,1)S(1)} %select_bitcast_fusion.2), channel_id=1, source_target_pairs={{4,0},{8,4},{12,8},{16,12},{20,16},{24,20},{28,24},{32,28},{36,32}... | collective-permute-start | bytes 98312 | tf_op jit(solution)/shard_map/ppermute | solution.py:12
  72.6 1.9 %collective-permute-start.9 = (bf16[64,8,8]{0,1,2:T(8,128)(2,1)S(1)}, bf16[64,8,8]{0,1,2:T(8,128)(2,1)S(1)}, u32[]{:S(2)}, u32[]{:S(2)}) collective-permute-start(bf16[64,8,8]{0,1,2:T(8,128)(2,1)S(1)} %select_bitcast_fusion.11), channel_id=1, source_target_pairs={{0,8},{4,12},{8,16},{12,20},{16,24},{20,28},{24,32},{28,36},{32,40... | collective-permute-start | bytes 24584 | tf_op jit(solution)/shard_map/ppermute | solution.py:12
  74.5 7.2 %collective-permute-start.10 = (bf16[64,8,8]{0,1,2:T(8,128)(2,1)S(1)}, bf16[64,8,8]{0,1,2:T(8,128)(2,1)S(1)}, u32[]{:S(2)}, u32[]{:S(2)}) collective-permute-start(bf16[64,8,8]{0,1,2:T(8,128)(2,1)S(1)} %select_bitcast_fusion.10), channel_id=1, source_target_pairs={{8,0},{12,4},{16,8},{20,12},{24,16},{28,20},{32,24},{36,28},{40,32... | collective-permute-start | bytes 24584 | tf_op jit(solution)/shard_map/ppermute | solution.py:12
  81.8 3.6 %collective-permute-start.13 = (bf16[64,8,8]{0,1,2:T(8,128)(2,1)S(1)}, bf16[64,8,8]{0,1,2:T(8,128)(2,1)S(1)}, u32[]{:S(2)}, u32[]{:S(2)}) collective-permute-start(bf16[64,8,8]{0,1,2:T(8,128)(2,1)S(1)} %collective-permute-done.11), channel_id=1, source_target_pairs={{0,1},{1,2},{2,3},{3,0},{4,5},{5,6},{6,7},{7,4},{8,9},{9,10},{10,1... | collective-permute-start | bytes 24584 | tf_op jit(solution)/shard_map/ppermute | solution.py:73
  85.8 1.8 %dynamic_update_slice.40 = bf16[64,8,32]{2,0,1:T(8,128)(2,1)S(1)} dynamic-update-slice(bf16[64,8,32]{2,0,1:T(8,128)(2,1)S(1)} %broadcast.134.clone.1, bf16[64,8,8]{2,0,1:T(8,128)(2,1)S(1)} %copy.187, s32[]{:T(128)} %constant.98.clone.1, s32[]{:T(128)} %constant.98.clone.1, s32[]{:T(128)S(6)} %select_n.226) | dynamic-update-slice | bytes 16388 | tf_op jit(solution)/shard_map/dynamic_update_slice | solution.py:69
  87.7 1.8 %dynamic_update_slice.41 = bf16[64,8,32]{2,0,1:T(8,128)(2,1)S(1)} dynamic-update-slice(bf16[64,8,32]{2,0,1:T(8,128)(2,1)S(1)} %dynamic_update_slice.40, bf16[64,8,8]{2,0,1:T(8,128)(2,1)S(1)} %copy.188, s32[]{:T(128)} %constant.98.clone.1, s32[]{:T(128)} %constant.98.clone.1, s32[]{:T(128)S(6)} %select_n.228) | dynamic-update-slice | bytes 16388 | tf_op jit(solution)/shard_map/dynamic_update_slice | solution.py:74
  90.5 1.8 %dynamic_update_slice.43 = bf16[64,8,32]{2,0,1:T(8,128)(2,1)S(1)} dynamic-update-slice(bf16[64,8,32]{2,0,1:T(8,128)(2,1)S(1)} %dynamic_update_slice.42, bf16[64,8,8]{2,0,1:T(8,128)(2,1)S(1)} %copy.190, s32[]{:T(128)} %constant.98.clone.1, s32[]{:T(128)} %constant.98.clone.1, s32[]{:T(128)S(6)} %select_n.232) | dynamic-update-slice | bytes 16388 | tf_op jit(solution)/shard_map/dynamic_update_slice | solution.py:74
  105.0 2.2 %collective-permute-start.18 = (bf16[64,8,8]{0,1,2:T(8,128)(2,1)S(1)}, bf16[64,8,8]{0,1,2:T(8,128)(2,1)S(1)}, u32[]{:S(2)}, u32[]{:S(2)}) collective-permute-start(bf16[64,8,8]{0,1,2:T(8,128)(2,1)S(1)} %select_bitcast_fusion.6), channel_id=1, source_target_pairs={{0,1},{1,2},{2,3},{3,0},{4,5},{5,6},{6,7},{7,4},{8,9},{9,10},{10,1... | collective-permute-start | bytes 24584 | tf_op jit(solution)/shard_map/ppermute | solution.py:73
  107.2 3.7 %collective-permute-start.19 = (bf16[64,8,8]{0,1,2:T(8,128)(2,1)S(1)}, bf16[64,8,8]{0,1,2:T(8,128)(2,1)S(1)}, u32[]{:S(2)}, u32[]{:S(2)}) collective-permute-start(bf16[64,8,8]{0,1,2:T(8,128)(2,1)S(1)} %select_bitcast_fusion.6), channel_id=1, source_target_pairs={{0,3},{1,0},{2,1},{3,2},{4,7},{5,4},{6,5},{7,6},{8,11},{9,8},{10,9... | collective-permute-start | bytes 24584 | tf_op jit(solution)/shard_map/ppermute | solution.py:78
  111.0 1.9 %collective-permute-start.14 = (bf16[64,8,32]{2,0,1:T(8,128)(2,1)S(1)}, bf16[64,8,32]{2,0,1:T(8,128)(2,1)S(1)}, u32[]{:S(2)}, u32[]{:S(2)}) collective-permute-start(bf16[64,8,32]{2,0,1:T(8,128)(2,1)S(1)} %select_bitcast_fusion.1), channel_id=1, source_target_pairs={{0,4},{4,8},{8,12},{12,16},{16,20},{20,24},{24,28},{28,32},{32,36}... | collective-permute-start | bytes 98312 | tf_op jit(solution)/shard_map/ppermute | solution.py:12
  113.1 7.0 %collective-permute-start.15 = (bf16[64,8,32]{2,0,1:T(8,128)(2,1)S(1)}, bf16[64,8,32]{2,0,1:T(8,128)(2,1)S(1)}, u32[]{:S(2)}, u32[]{:S(2)}) collective-permute-start(bf16[64,8,32]{2,0,1:T(8,128)(2,1)S(1)} %select_bitcast_fusion), channel_id=1, source_target_pairs={{4,0},{8,4},{12,8},{16,12},{20,16},{24,20},{28,24},{32,28},{36,32}... | collective-permute-start | bytes 98312 | tf_op jit(solution)/shard_map/ppermute | solution.py:12
  120.4 1.9 %collective-permute-start.16 = (bf16[64,8,8]{0,1,2:T(8,128)(2,1)S(1)}, bf16[64,8,8]{0,1,2:T(8,128)(2,1)S(1)}, u32[]{:S(2)}, u32[]{:S(2)}) collective-permute-start(bf16[64,8,8]{0,1,2:T(8,128)(2,1)S(1)} %select_bitcast_fusion.8), channel_id=1, source_target_pairs={{0,8},{4,12},{8,16},{12,20},{16,24},{20,28},{24,32},{28,36},{32,40... | collective-permute-start | bytes 24584 | tf_op jit(solution)/shard_map/ppermute | solution.py:12
  122.4 7.2 %collective-permute-start.17 = (bf16[64,8,8]{0,1,2:T(8,128)(2,1)S(1)}, bf16[64,8,8]{0,1,2:T(8,128)(2,1)S(1)}, u32[]{:S(2)}, u32[]{:S(2)}) collective-permute-start(bf16[64,8,8]{0,1,2:T(8,128)(2,1)S(1)} %select_bitcast_fusion.7), channel_id=1, source_target_pairs={{8,0},{12,4},{16,8},{20,12},{24,16},{28,20},{32,24},{36,28},{40,32... | collective-permute-start | bytes 24584 | tf_op jit(solution)/shard_map/ppermute | solution.py:12
  129.6 3.6 %collective-permute-start.20 = (bf16[64,8,8]{0,1,2:T(8,128)(2,1)S(1)}, bf16[64,8,8]{0,1,2:T(8,128)(2,1)S(1)}, u32[]{:S(2)}, u32[]{:S(2)}) collective-permute-start(bf16[64,8,8]{0,1,2:T(8,128)(2,1)S(1)} %collective-permute-done.18), channel_id=1, source_target_pairs={{0,1},{1,2},{2,3},{3,0},{4,5},{5,6},{6,7},{7,4},{8,9},{9,10},{10,1... | collective-permute-start | bytes 24584 | tf_op jit(solution)/shard_map/ppermute | solution.py:73
  133.7 1.8 %dynamic_update_slice.44 = bf16[64,8,32]{2,0,1:T(8,128)(2,1)S(1)} dynamic-update-slice(bf16[64,8,32]{2,0,1:T(8,128)(2,1)S(1)} %broadcast.134, bf16[64,8,8]{2,0,1:T(8,128)(2,1)S(1)} %copy.221, s32[]{:T(128)} %constant.98.clone.1, s32[]{:T(128)} %constant.98.clone.1, s32[]{:T(128)S(6)} %select_n.226) | dynamic-update-slice | bytes 16388 | tf_op jit(solution)/shard_map/dynamic_update_slice | solution.py:69
  135.6 1.8 %dynamic_update_slice.45 = bf16[64,8,32]{2,0,1:T(8,128)(2,1)S(1)} dynamic-update-slice(bf16[64,8,32]{2,0,1:T(8,128)(2,1)S(1)} %dynamic_update_slice.44, bf16[64,8,8]{2,0,1:T(8,128)(2,1)S(1)} %copy.222, s32[]{:T(128)} %constant.98.clone.1, s32[]{:T(128)} %constant.98.clone.1, s32[]{:T(128)S(6)} %select_n.228) | dynamic-update-slice | bytes 16388 | tf_op jit(solution)/shard_map/dynamic_update_slice | solution.py:74
  138.4 1.8 %dynamic_update_slice.47 = bf16[64,8,32]{2,0,1:T(8,128)(2,1)S(1)} dynamic-update-slice(bf16[64,8,32]{2,0,1:T(8,128)(2,1)S(1)} %dynamic_update_slice.46, bf16[64,8,8]{2,0,1:T(8,128)(2,1)S(1)} %copy.224, s32[]{:T(128)} %constant.98.clone.1, s32[]{:T(128)} %constant.98.clone.1, s32[]{:T(128)S(6)} %select_n.232) | dynamic-update-slice | bytes 16388 | tf_op jit(solution)/shard_map/dynamic_update_slice | solution.py:74
  150.1 2.5 %collective-permute-start.21 = (bf16[64,8,16]{2,0,1:T(8,128)(2,1)S(1)}, bf16[64,8,16]{2,0,1:T(8,128)(2,1)S(1)}, u32[]{:S(2)}, u32[]{:S(2)}) collective-permute-start(bf16[64,8,16]{2,0,1:T(8,128)(2,1)S(1)} %fusion.32), channel_id=1, source_target_pairs={{0,1},{1,0},{2,3},{3,2},{4,5},{5,4},{6,7},{7,6},{8,9},{9,8},{10,11... | collective-permute-start | bytes 49160 | tf_op jit(solution)/shard_map/ppermute | solution.py:22
  153.4 3.5 %collective-permute-done.21 = bf16[64,8,16]{2,0,1:T(8,128)(2,1)S(1)} collective-permute-done((bf16[64,8,16]{2,0,1:T(8,128)(2,1)S(1)}, bf16[64,8,16]{2,0,1:T(8,128)(2,1)S(1)}, u32[]{:S(2)}, u32[]{:S(2)}) %collective-permute-start.21) | collective-permute-done | bytes 16416 | tf_op jit(solution)/shard_map/ppermute | solution.py:22
  (278 shorter events, 52.8 us)
Async XLA Ops:
  0.6 157.7 %copy-start = (bf16[64,64]{1,0:T(8,128)(2,1)S(1)}, bf16[64,64]{1,0:T(8,128)(2,1)}, u32[]{:S(2)}) copy-start(bf16[64,64]{1,0:T(8,128)(2,1)} %param.25) | copy-start | bytes 24580
  2.6 7.7 %copy-start.8 = (s32[2,32]{1,0:T(2,128)S(1)}, s32[2,32]{1,0:T(2,128)}, u32[]{:S(2)}) copy-start(s32[2,32]{1,0:T(2,128)} %param.29) | copy-start | bytes 772
  4.5 20.9 %collective-permute-start.4 = (bf16[64,8,8]{0,1,2:T(8,128)(2,1)S(1)}, bf16[64,8,8]{0,1,2:T(8,128)(2,1)S(1)}, u32[]{:S(2)}, u32[]{:S(2)}) collective-permute-start(bf16[64,8,8]{0,1,2:T(8,128)(2,1)S(1)} %select_bitcast_fusion.12), channel_id=1, source_target_pairs={{0,1},{1,2},{2,3},{3,0},{4,5},{5,6},{6,7},{7,4},{8,9},{9,10},{10,1... | collective-permute-start | bytes 24584 | tf_op jit(solution)/shard_map/ppermute | solution.py:73
  6.9 25.8 %collective-permute-start.5 = (bf16[64,8,8]{0,1,2:T(8,128)(2,1)S(1)}, bf16[64,8,8]{0,1,2:T(8,128)(2,1)S(1)}, u32[]{:S(2)}, u32[]{:S(2)}) collective-permute-start(bf16[64,8,8]{0,1,2:T(8,128)(2,1)S(1)} %select_bitcast_fusion.12), channel_id=1, source_target_pairs={{0,3},{1,0},{2,1},{3,2},{4,7},{5,4},{6,5},{7,6},{8,11},{9,8},{10,9... | collective-permute-start | bytes 24584 | tf_op jit(solution)/shard_map/ppermute | solution.py:78
  11.0 9.9 %copy-start.9 = (s32[2,8]{1,0:T(2,128)S(1)}, s32[2,8]{1,0:T(2,128)}, u32[]{:S(2)}) copy-start(s32[2,8]{1,0:T(2,128)} %param.30) | copy-start | bytes 196
  11.1 12.3 %copy-start.10 = (s32[16]{0:T(128)S(1)}, s32[16]{0:T(128)}, u32[]{:S(2)}) copy-start(s32[16]{0:T(128)} %param.33) | copy-start | bytes 196
  11.2 12.4 %copy-start.11 = (s32[128]{0:T(128)S(1)}, s32[128]{0:T(128)}, u32[]{:S(2)}) copy-start(s32[128]{0:T(128)} %param.32) | copy-start | bytes 1540
  11.2 31.8 %collective-permute-start = (bf16[64,8,32]{2,0,1:T(8,128)(2,1)S(1)}, bf16[64,8,32]{2,0,1:T(8,128)(2,1)S(1)}, u32[]{:S(2)}, u32[]{:S(2)}) collective-permute-start(bf16[64,8,32]{2,0,1:T(8,128)(2,1)S(1)} %select_bitcast_fusion.5), channel_id=1, source_target_pairs={{0,4},{4,8},{8,12},{12,16},{16,20},{20,24},{24,28},{28,32},{32,36}... | collective-permute-start | bytes 98312 | tf_op jit(solution)/shard_map/ppermute | solution.py:12
  13.9 29.1 %collective-permute-start.1 = (bf16[64,8,32]{2,0,1:T(8,128)(2,1)S(1)}, bf16[64,8,32]{2,0,1:T(8,128)(2,1)S(1)}, u32[]{:S(2)}, u32[]{:S(2)}) collective-permute-start(bf16[64,8,32]{2,0,1:T(8,128)(2,1)S(1)} %select_bitcast_fusion.4), channel_id=1, source_target_pairs={{4,0},{8,4},{12,8},{16,12},{20,16},{24,20},{28,24},{32,28},{36,32}... | collective-permute-start | bytes 98312 | tf_op jit(solution)/shard_map/ppermute | solution.py:12
  21.5 19.3 %collective-permute-start.2 = (bf16[64,8,8]{0,1,2:T(8,128)(2,1)S(1)}, bf16[64,8,8]{0,1,2:T(8,128)(2,1)S(1)}, u32[]{:S(2)}, u32[]{:S(2)}) collective-permute-start(bf16[64,8,8]{0,1,2:T(8,128)(2,1)S(1)} %select_bitcast_fusion.14), channel_id=1, source_target_pairs={{0,8},{4,12},{8,16},{12,20},{16,24},{20,28},{24,32},{28,36},{32,40... | collective-permute-start | bytes 24584 | tf_op jit(solution)/shard_map/ppermute | solution.py:12
  23.6 1.3 copy-start.7
  23.6 1.4 copy-start.3
  23.6 1.4 copy-start.5
  25.4 15.5 %collective-permute-start.3 = (bf16[64,8,8]{0,1,2:T(8,128)(2,1)S(1)}, bf16[64,8,8]{0,1,2:T(8,128)(2,1)S(1)}, u32[]{:S(2)}, u32[]{:S(2)}) collective-permute-start(bf16[64,8,8]{0,1,2:T(8,128)(2,1)S(1)} %select_bitcast_fusion.13), channel_id=1, source_target_pairs={{8,0},{12,4},{16,8},{20,12},{24,16},{28,20},{32,24},{36,28},{40,32... | collective-permute-start | bytes 24584 | tf_op jit(solution)/shard_map/ppermute | solution.py:12
  32.7 8.4 %collective-permute-start.6 = (bf16[64,8,8]{0,1,2:T(8,128)(2,1)S(1)}, bf16[64,8,8]{0,1,2:T(8,128)(2,1)S(1)}, u32[]{:S(2)}, u32[]{:S(2)}) collective-permute-start(bf16[64,8,8]{0,1,2:T(8,128)(2,1)S(1)} %collective-permute-done.4), channel_id=1, source_target_pairs={{0,1},{1,2},{2,3},{3,0},{4,5},{5,6},{6,7},{7,4},{8,9},{9,10},{10,1... | collective-permute-start | bytes 24584 | tf_op jit(solution)/shard_map/ppermute | solution.py:73
  51.5 1.0 copy-start.1
  52.7 1.0 copy-start.2
  57.2 17.4 %collective-permute-start.11 = (bf16[64,8,8]{0,1,2:T(8,128)(2,1)S(1)}, bf16[64,8,8]{0,1,2:T(8,128)(2,1)S(1)}, u32[]{:S(2)}, u32[]{:S(2)}) collective-permute-start(bf16[64,8,8]{0,1,2:T(8,128)(2,1)S(1)} %select_bitcast_fusion.9), channel_id=1, source_target_pairs={{0,1},{1,2},{2,3},{3,0},{4,5},{5,6},{6,7},{7,4},{8,9},{9,10},{10,1... | collective-permute-start | bytes 24584 | tf_op jit(solution)/shard_map/ppermute | solution.py:73
  59.4 22.4 %collective-permute-start.12 = (bf16[64,8,8]{0,1,2:T(8,128)(2,1)S(1)}, bf16[64,8,8]{0,1,2:T(8,128)(2,1)S(1)}, u32[]{:S(2)}, u32[]{:S(2)}) collective-permute-start(bf16[64,8,8]{0,1,2:T(8,128)(2,1)S(1)} %select_bitcast_fusion.9), channel_id=1, source_target_pairs={{0,3},{1,0},{2,1},{3,2},{4,7},{5,4},{6,5},{7,6},{8,11},{9,8},{10,9... | collective-permute-start | bytes 24584 | tf_op jit(solution)/shard_map/ppermute | solution.py:78
  63.2 29.1 %collective-permute-start.7 = (bf16[64,8,32]{2,0,1:T(8,128)(2,1)S(1)}, bf16[64,8,32]{2,0,1:T(8,128)(2,1)S(1)}, u32[]{:S(2)}, u32[]{:S(2)}) collective-permute-start(bf16[64,8,32]{2,0,1:T(8,128)(2,1)S(1)} %select_bitcast_fusion.3), channel_id=1, source_target_pairs={{0,4},{4,8},{8,12},{12,16},{16,20},{20,24},{24,28},{28,32},{32,36}... | collective-permute-start | bytes 98312 | tf_op jit(solution)/shard_map/ppermute | solution.py:12
  65.3 27.0 %collective-permute-start.8 = (bf16[64,8,32]{2,0,1:T(8,128)(2,1)S(1)}, bf16[64,8,32]{2,0,1:T(8,128)(2,1)S(1)}, u32[]{:S(2)}, u32[]{:S(2)}) collective-permute-start(bf16[64,8,32]{2,0,1:T(8,128)(2,1)S(1)} %select_bitcast_fusion.2), channel_id=1, source_target_pairs={{4,0},{8,4},{12,8},{16,12},{20,16},{24,20},{28,24},{32,28},{36,32}... | collective-permute-start | bytes 98312 | tf_op jit(solution)/shard_map/ppermute | solution.py:12
  72.6 17.5 %collective-permute-start.9 = (bf16[64,8,8]{0,1,2:T(8,128)(2,1)S(1)}, bf16[64,8,8]{0,1,2:T(8,128)(2,1)S(1)}, u32[]{:S(2)}, u32[]{:S(2)}) collective-permute-start(bf16[64,8,8]{0,1,2:T(8,128)(2,1)S(1)} %select_bitcast_fusion.11), channel_id=1, source_target_pairs={{0,8},{4,12},{8,16},{12,20},{16,24},{20,28},{24,32},{28,36},{32,40... | collective-permute-start | bytes 24584 | tf_op jit(solution)/shard_map/ppermute | solution.py:12
  74.5 15.7 %collective-permute-start.10 = (bf16[64,8,8]{0,1,2:T(8,128)(2,1)S(1)}, bf16[64,8,8]{0,1,2:T(8,128)(2,1)S(1)}, u32[]{:S(2)}, u32[]{:S(2)}) collective-permute-start(bf16[64,8,8]{0,1,2:T(8,128)(2,1)S(1)} %select_bitcast_fusion.10), channel_id=1, source_target_pairs={{8,0},{12,4},{16,8},{20,12},{24,16},{28,20},{32,24},{36,28},{40,32... | collective-permute-start | bytes 24584 | tf_op jit(solution)/shard_map/ppermute | solution.py:12
  81.8 8.6 %collective-permute-start.13 = (bf16[64,8,8]{0,1,2:T(8,128)(2,1)S(1)}, bf16[64,8,8]{0,1,2:T(8,128)(2,1)S(1)}, u32[]{:S(2)}, u32[]{:S(2)}) collective-permute-start(bf16[64,8,8]{0,1,2:T(8,128)(2,1)S(1)} %collective-permute-done.11), channel_id=1, source_target_pairs={{0,1},{1,2},{2,3},{3,0},{4,5},{5,6},{6,7},{7,4},{8,9},{9,10},{10,1... | collective-permute-start | bytes 24584 | tf_op jit(solution)/shard_map/ppermute | solution.py:73
  105.0 17.4 %collective-permute-start.18 = (bf16[64,8,8]{0,1,2:T(8,128)(2,1)S(1)}, bf16[64,8,8]{0,1,2:T(8,128)(2,1)S(1)}, u32[]{:S(2)}, u32[]{:S(2)}) collective-permute-start(bf16[64,8,8]{0,1,2:T(8,128)(2,1)S(1)} %select_bitcast_fusion.6), channel_id=1, source_target_pairs={{0,1},{1,2},{2,3},{3,0},{4,5},{5,6},{6,7},{7,4},{8,9},{9,10},{10,1... | collective-permute-start | bytes 24584 | tf_op jit(solution)/shard_map/ppermute | solution.py:73
  107.2 22.5 %collective-permute-start.19 = (bf16[64,8,8]{0,1,2:T(8,128)(2,1)S(1)}, bf16[64,8,8]{0,1,2:T(8,128)(2,1)S(1)}, u32[]{:S(2)}, u32[]{:S(2)}) collective-permute-start(bf16[64,8,8]{0,1,2:T(8,128)(2,1)S(1)} %select_bitcast_fusion.6), channel_id=1, source_target_pairs={{0,3},{1,0},{2,1},{3,2},{4,7},{5,4},{6,5},{7,6},{8,11},{9,8},{10,9... | collective-permute-start | bytes 24584 | tf_op jit(solution)/shard_map/ppermute | solution.py:78
  111.0 29.1 %collective-permute-start.14 = (bf16[64,8,32]{2,0,1:T(8,128)(2,1)S(1)}, bf16[64,8,32]{2,0,1:T(8,128)(2,1)S(1)}, u32[]{:S(2)}, u32[]{:S(2)}) collective-permute-start(bf16[64,8,32]{2,0,1:T(8,128)(2,1)S(1)} %select_bitcast_fusion.1), channel_id=1, source_target_pairs={{0,4},{4,8},{8,12},{12,16},{16,20},{20,24},{24,28},{28,32},{32,36}... | collective-permute-start | bytes 98312 | tf_op jit(solution)/shard_map/ppermute | solution.py:12
  113.1 27.0 %collective-permute-start.15 = (bf16[64,8,32]{2,0,1:T(8,128)(2,1)S(1)}, bf16[64,8,32]{2,0,1:T(8,128)(2,1)S(1)}, u32[]{:S(2)}, u32[]{:S(2)}) collective-permute-start(bf16[64,8,32]{2,0,1:T(8,128)(2,1)S(1)} %select_bitcast_fusion), channel_id=1, source_target_pairs={{4,0},{8,4},{12,8},{16,12},{20,16},{24,20},{28,24},{32,28},{36,32}... | collective-permute-start | bytes 98312 | tf_op jit(solution)/shard_map/ppermute | solution.py:12
  120.4 17.5 %collective-permute-start.16 = (bf16[64,8,8]{0,1,2:T(8,128)(2,1)S(1)}, bf16[64,8,8]{0,1,2:T(8,128)(2,1)S(1)}, u32[]{:S(2)}, u32[]{:S(2)}) collective-permute-start(bf16[64,8,8]{0,1,2:T(8,128)(2,1)S(1)} %select_bitcast_fusion.8), channel_id=1, source_target_pairs={{0,8},{4,12},{8,16},{12,20},{16,24},{20,28},{24,32},{28,36},{32,40... | collective-permute-start | bytes 24584 | tf_op jit(solution)/shard_map/ppermute | solution.py:12
  122.4 15.7 %collective-permute-start.17 = (bf16[64,8,8]{0,1,2:T(8,128)(2,1)S(1)}, bf16[64,8,8]{0,1,2:T(8,128)(2,1)S(1)}, u32[]{:S(2)}, u32[]{:S(2)}) collective-permute-start(bf16[64,8,8]{0,1,2:T(8,128)(2,1)S(1)} %select_bitcast_fusion.7), channel_id=1, source_target_pairs={{8,0},{12,4},{16,8},{20,12},{24,16},{28,20},{32,24},{36,28},{40,32... | collective-permute-start | bytes 24584 | tf_op jit(solution)/shard_map/ppermute | solution.py:12
  129.6 8.6 %collective-permute-start.20 = (bf16[64,8,8]{0,1,2:T(8,128)(2,1)S(1)}, bf16[64,8,8]{0,1,2:T(8,128)(2,1)S(1)}, u32[]{:S(2)}, u32[]{:S(2)}) collective-permute-start(bf16[64,8,8]{0,1,2:T(8,128)(2,1)S(1)} %collective-permute-done.18), channel_id=1, source_target_pairs={{0,1},{1,2},{2,3},{3,0},{4,5},{5,6},{6,7},{7,4},{8,9},{9,10},{10,1... | collective-permute-start | bytes 24584 | tf_op jit(solution)/shard_map/ppermute | solution.py:73
  150.1 6.9 %collective-permute-start.21 = (bf16[64,8,16]{2,0,1:T(8,128)(2,1)S(1)}, bf16[64,8,16]{2,0,1:T(8,128)(2,1)S(1)}, u32[]{:S(2)}, u32[]{:S(2)}) collective-permute-start(bf16[64,8,16]{2,0,1:T(8,128)(2,1)S(1)} %fusion.32), channel_id=1, source_target_pairs={{0,1},{1,0},{2,3},{3,2},{4,5},{5,4},{6,7},{7,6},{8,9},{9,8},{10,11... | collective-permute-start | bytes 49160 | tf_op jit(solution)/shard_map/ppermute | solution.py:22
  (2 other events, 1.5 us)
